TPU v7x, 32 devices: a whole 2x2x4 slice. The times are simulated.
32 devices in a mesh: row: 8 (over y, x, core), col: 4 (over z).
Axes of the slice: x: 2, y: 2, z: 4, core: 2. Of those that a mesh axis runs over, the one named last changes fastest.
Arguments:
- matrix: float32 [16384, 16384], P('row', 'col'), may hold values from -9 to 9
- vectors: float32 [16384, 128], P('row'), may hold values from -0.125 to 0.125
- tfactor: float32 [128, 128], replicated, may hold values from -1 to 2, as said below
Outputs:
- updated: float32 [16384, 16384], P('row', 'col')
Inputs may be any that keep to these rules, and one draw needn't show every extreme that they name: tfactor is upper triangular with its diagonal between 0.7 and 1.4.
All inputs are finite; a program needn't handle non-finite values.
Results may differ from a plain program's by a relative error of at most 0.000094.
Values sent between devices are 32-bit elements; how exact they have to be, the bound alone decides.
A program may use at most 192 MiB of HBM per device.

v0:
```python
import jax
import jax.numpy as jnp
from jax import lax
from jax.sharding import PartitionSpec as P


def product(left, right):
    return jnp.dot(left, right, precision=lax.Precision.HIGHEST, preferred_element_type=jnp.float32)


def inner_product(left, right):
    return lax.dot_general(
        left,
        right,
        (((0,), (0,)), ((), ())),
        precision=lax.Precision.HIGHEST,
        preferred_element_type=jnp.float32,
    )


def outer_product(left, right):
    return lax.dot_general(
        left,
        right,
        (((1,), (1,)), ((), ())),
        precision=lax.Precision.HIGHEST,
        preferred_element_type=jnp.float32,
    )


def to_columns(panel_rows):
    rows_here = panel_rows.shape[0]
    row_count = lax.axis_size("row")
    blocks_per = row_count // lax.axis_size("col")
    col_index = lax.axis_index("col")
    gathered = lax.all_gather(panel_rows, "row", axis=0, tiled=True)
    return lax.dynamic_slice_in_dim(
        gathered, col_index * (blocks_per * rows_here), blocks_per * rows_here, 0
    )


def shards(matrix, vectors, tfactor):
    vec_cols = to_columns(vectors)
    x_rows = lax.psum(product(matrix, vec_cols), "col")
    y_rows = product(x_rows, tfactor)
    cross_terms = lax.psum(inner_product(vectors, y_rows), "row")
    coupling = inner_product(tfactor, cross_terms)
    w_rows = y_rows - 0.5 * product(vectors, coupling)
    w_cols = to_columns(w_rows)
    return matrix - outer_product(vectors, w_cols) - outer_product(w_rows, vec_cols)


def solution(mesh):
    in_specs = (P("row", "col"), P("row", None), P())
    out_specs = P("row", "col")
    return jax.shard_map(shards, mesh=mesh, in_specs=in_specs, out_specs=out_specs, check_vma=False)
```

profile of v0, /device:TPU:3, one launch (start us, length us, event | category | flops | bytes accessed | tf_op | source)
XLA Modules:
  0.0 362.3 jit_solution(2363091480754397307)
XLA Ops:
  6.5 0.0 copy-start
  6.5 0.0 all-gather.3.cloned.1.call-start
  6.5 0.7 all-gather.3.cloned.1.call-update
  7.3 0.0 all-reduce.3.cloned.1.call-start
  7.3 58.0 %all-gather.3.cloned.1.call-done = f32[16384,128]{1,0:T(8,128)} async-done(((f32[2048,128]{1,0:T(8,128)}), f32[16384,128]{1,0:T(8,128)}) %all-gather.3.cloned.1.call-update) | async-done | bytes 8388624 | tf_op jit(solution)/shard_map/all_gather | solution.py:36
  65.3 42.1 %convolution_bitcast_fusion = f32[2048,128]{0,1:T(8,128)} fusion(f32[2048,4096]{1,0:T(8,128)} %param.3, f32[16384,128]{1,0:T(8,128)} %all-gather.3.cloned.1.call-done, s32[]{:T(128)S(6)} %select_n.4), kind=kOutput, calls=%fused_computation.2 | convolution fusion | flops 12884901888 | bytes 36700164 | tf_op jit(solution)/shard_map/dot_general | solution.py:8
  107.4 0.0 all-reduce.3.cloned.1.call-update
  107.4 0.0 all-reduce.5.cloned.1.call-start
  107.5 51.7 %all-reduce.3.cloned.1.call-done = f32[2048,128]{0,1:T(8,128)} async-done(((f32[2048,128]{0,1:T(8,128)}), f32[2048,128]{0,1:T(8,128)}) %all-reduce.3.cloned.1.call-update) | async-done | bytes 1048592 | tf_op jit(solution)/shard_map/psum | solution.py:44
  159.2 0.0 copy-done
  159.2 3.0 fusion.10
  162.2 0.0 copy-done.2
  162.2 2.4 convolution_bitcast_fusion.1
  164.7 0.0 all-reduce.5.cloned.1.call-update
  164.7 0.0 all-gather.5.cloned.1.call-start
  164.7 50.1 %all-reduce.5.cloned.1.call-done = f32[128,128]{0,1:T(8,128)} async-done(((f32[128,128]{0,1:T(8,128)}), f32[128,128]{0,1:T(8,128)}) %all-reduce.5.cloned.1.call-update) | async-done | bytes 65552 | tf_op jit(solution)/shard_map/psum | solution.py:46
  214.8 1.0 fusion.11
  215.9 2.0 fusion.2
  217.9 0.0 all-gather.5.cloned.1.call-update
  217.9 33.8 %copy.5 = f32[2048,4096]{0,1:T(8,128)} copy(f32[2048,4096]{1,0:T(8,128)} %param.3) | data formatting | bytes 67108864 | tf_op args[0]
  251.7 0.0 copy-done.3
  251.7 31.3 %fusion.4 = f32[2048,4096]{0,1:T(8,128)} fusion(f32[2048,128]{1,0:T(8,128)S(1)} %copy-done.3, f32[16384,128]{1,0:T(8,128)} %all-gather.3.cloned.1.call-done, s32[]{:T(128)S(6)} %select_n.4), kind=kOutput, calls=%fused_computation.7 | convolution fusion | flops 12884901888 | bytes 36700164 | tf_op jit(solution)/shard_map/dot_general | solution.py:22
  283.0 41.7 %fusion = f32[2048,4096]{0,1:T(8,128)} fusion(f32[2048,4096]{0,1:T(8,128)} %fusion.4, f32[2048,4096]{0,1:T(8,128)} %copy.5, f32[2048,128]{1,0:T(8,128)S(1)} %copy-done.2, f32[16384,128]{1,0:T(8,128)} %all-gather.5.cloned.1.call-done, s32[]{:T(128)S(6)} %select_n.4), kind=kOutput, calls=%fused_computation.1 | convolution fusion | flops 12901679104 | bytes 103809024 | tf_op jit(solution)/shard_map/dot_general | solution.py:22
  324.7 31.1 %copy.7 = f32[2048,4096]{1,0:T(8,128)} copy(f32[2048,4096]{0,1:T(8,128)} %fusion) | data formatting | bytes 67108864 | tf_op jit(solution)/shard_map/sub | solution.py:50
  (5 shorter events, 0.0 us)
Async XLA Ops:
  6.5 152.6 %copy-start = (f32[128,128]{1,0:T(8,128)S(1)}, f32[128,128]{1,0:T(8,128)}, u32[]{:S(2)}) copy-start(f32[128,128]{1,0:T(8,128)} %param.5) | copy-start | bytes 196612
  6.5 155.7 %copy-start.2 = (f32[2048,128]{1,0:T(8,128)S(1)}, f32[2048,128]{1,0:T(8,128)}, u32[]{:S(2)}) copy-start(f32[2048,128]{1,0:T(8,128)} %param.4) | copy-start | bytes 3145732
  6.5 58.8 %all-gather.3.cloned.1.call-start = ((), (), s32[]{:S(2)}) async-start(), calls=%async_computation | async-start | bytes 9437184 | tf_op jit(solution)/shard_map/all_gather | solution.py:36
  7.3 151.9 %all-reduce.3.cloned.1.call-start = ((), (), s32[]{:S(2)}) async-start(), calls=%async_computation.1 | async-start | bytes 2097152 | tf_op jit(solution)/shard_map/psum | solution.py:44
  107.4 107.4 %all-reduce.5.cloned.1.call-start = ((), (), s32[]{:S(2)}) async-start(), calls=%async_computation.2 | async-start | bytes 131072 | tf_op jit(solution)/shard_map/psum | solution.py:46
  164.7 118.3 %all-gather.5.cloned.1.call-start = ((), (), s32[]{:S(2)}) async-start(), calls=%async_computation.3 | async-start | bytes 9437184 | tf_op jit(solution)/shard_map/all_gather | solution.py:36
  217.9 33.8 %copy-start.3 = (f32[2048,128]{1,0:T(8,128)S(1)}, f32[2048,128]{1,0:T(8,128)}, u32[]{:S(2)}) copy-start(f32[2048,128]{1,0:T(8,128)} %fusion.2) | copy-start | bytes 3145732
  283.0 72.8 %copy-start.1 = (f32[128,128]{1,0:T(8,128)S(1)}, f32[128,128]{1,0:T(8,128)}, u32[]{:S(2)}) copy-start(f32[128,128]{1,0:T(8,128)} %param.5) | copy-start | bytes 196612
Sparse Core Ops, SparseCore 0:
  9.2 56.0 all-gather.2
  107.5 51.5 all-reduce.2
  164.8 49.9 all-reduce.4
  218.0 55.8 all-gather.4
where the time goes:
time: 367 us; the launch traced here: 362 us
  waiting for transfers between devices  161 us (44%)
  matrix products  124 us (34%)
  local copies, waits for them, and re-layouts  64.9 us (18%)
  between operations  13.2 us (4%)
    dot_general x2, matrix products, outer_product(): lax.dot_general(left, right, (((1,), (1,)), ((), ())), precision=lax.Prec...  73 us
    all_gather x2, waiting for transfers between devices, to_columns(): gathered = lax.all_gather(panel_rows, 'row', axis=0, tiled=True)  58 us
    psum x1, waiting for transfers between devices, shards(): x_rows = lax.psum(product(matrix, vec_cols), 'col')  51.7 us
    psum x1, waiting for transfers between devices, shards(): cross_terms = lax.psum(inner_product(vectors, y_rows), 'row')  50.1 us
    dot_general x3, matrix products, product(): jnp.dot(left, right, precision=lax.Precision.HIGHEST, preferred_element_t...  47.1 us
    unnamed x9, local copies, waits for them, and re-layouts  33.8 us
    sub x1, local copies, waits for them, and re-layouts, shards(): matrix - outer_product(vectors, w_cols) - outer_product(w_rows, vec_cols)  31.1 us
  transfers between devices with their start and end apart: 4, of which 3 were waited for; matrix products, arithmetic and copies ran while one was open for 18% of the time, Pallas kernels for 0%

commit v1 on v0

v1 whole, which is shorter than its diff:
```python
import functools

import jax
import jax.numpy as jnp
from jax import lax
from jax.experimental import pallas as pl
from jax.experimental.pallas import tpu as pltpu
from jax.sharding import PartitionSpec as P

NT = (((1,), (1,)), ((), ()))
TN = (((0,), (0,)), ((), ()))


def product(left, right):
    return jnp.dot(left, right, precision=lax.Precision.HIGHEST, preferred_element_type=jnp.float32)


def inner_product(left, right):
    return lax.dot_general(
        left, right, TN, precision=lax.Precision.HIGHEST, preferred_element_type=jnp.float32
    )


def split(values):
    high = values.astype(jnp.bfloat16)
    low = (values - high.astype(jnp.float32)).astype(jnp.bfloat16)
    return high, low


def product_kernel(a_ref, v_ref, x_ref, v2):
    nb = v_ref.shape[1]

    @pl.when(pl.program_id(0) == 0)
    def _():
        high, low = split(v_ref[...])
        v2[:, :nb] = high
        v2[:, nb:] = low

    high, low = split(a_ref[...])
    both = jnp.dot(high, v2[...], preferred_element_type=jnp.float32)
    both += jnp.dot(low, v2[...], preferred_element_type=jnp.float32)
    x_ref[...] = both[:, :nb] + both[:, nb:]


def tile_product(matrix, vec_cols):
    rows, columns = matrix.shape
    nb = vec_cols.shape[1]
    block = min(256, rows)
    return pl.pallas_call(
        product_kernel,
        grid=(rows // block,),
        in_specs=[
            pl.BlockSpec((block, columns), lambda i: (i, 0)),
            pl.BlockSpec((columns, nb), lambda i: (0, 0)),
        ],
        out_specs=pl.BlockSpec((block, nb), lambda i: (i, 0)),
        out_shape=jax.ShapeDtypeStruct((rows, nb), jnp.float32),
        scratch_shapes=[pltpu.VMEM((columns, 2 * nb), jnp.bfloat16)],
        compiler_params=pltpu.CompilerParams(vmem_limit_bytes=56 << 20),
        name="tile_product",
    )(matrix, vec_cols)


def update_kernel(a_ref, vr_ref, wr_ref, vc_ref, wc_ref, out_ref, right):
    nb = vr_ref.shape[1]
    columns = a_ref.shape[1]
    wide = min(512, columns)

    @pl.when(pl.program_id(0) == 0)
    def _():
        for at, ref in ((0, wc_ref), (nb, vc_ref)):
            high, low = split(ref[...])
            right[:, at : at + nb] = high
            right[:, 2 * nb + at : 3 * nb + at] = low
            right[:, 4 * nb + at : 5 * nb + at] = high

    v_high, v_low = split(vr_ref[...])
    w_high, w_low = split(wr_ref[...])
    left = jnp.concatenate([v_high, w_high, v_high, w_high, v_low, w_low], axis=1)
    for at in range(0, columns, wide):
        change = lax.dot_general(
            left, right[at : at + wide, :], NT, preferred_element_type=jnp.float32
        )
        out_ref[:, at : at + wide] = a_ref[:, at : at + wide] - change


def tile_update(matrix, vectors, w_rows, vec_cols, w_cols):
    rows, columns = matrix.shape
    nb = vectors.shape[1]
    block = min(256, rows)
    return pl.pallas_call(
        update_kernel,
        grid=(rows // block,),
        in_specs=[
            pl.BlockSpec((block, columns), lambda i: (i, 0)),
            pl.BlockSpec((block, nb), lambda i: (i, 0)),
            pl.BlockSpec((block, nb), lambda i: (i, 0)),
            pl.BlockSpec((columns, nb), lambda i: (0, 0)),
            pl.BlockSpec((columns, nb), lambda i: (0, 0)),
        ],
        out_specs=pl.BlockSpec((block, columns), lambda i: (i, 0)),
        out_shape=jax.ShapeDtypeStruct((rows, columns), jnp.float32),
        scratch_shapes=[pltpu.VMEM((columns, 6 * nb), jnp.bfloat16)],
        compiler_params=pltpu.CompilerParams(vmem_limit_bytes=56 << 20),
        name="tile_update",
    )(matrix, vectors, w_rows, vec_cols, w_cols)


def to_columns(panel_rows):
    rows_here = panel_rows.shape[0]
    blocks_per = lax.axis_size("row") // lax.axis_size("col")
    gathered = lax.all_gather(panel_rows, "row", axis=0, tiled=True)
    return lax.dynamic_slice_in_dim(
        gathered, lax.axis_index("col") * (blocks_per * rows_here), blocks_per * rows_here, 0
    )


def shards(matrix, vectors, tfactor):
    vec_cols = to_columns(vectors)
    x_part = tile_product(matrix, vec_cols)
    x_rows = lax.psum(x_part, "col")
    cross = lax.psum(inner_product(vectors, x_part), ("row", "col"))
    middle = 0.5 * product(inner_product(tfactor, cross), tfactor)
    x_cols = to_columns(x_rows)
    w_rows = product(x_rows, tfactor) - product(vectors, middle)
    w_cols = product(x_cols, tfactor) - product(vec_cols, middle)
    return tile_update(matrix, vectors, w_rows, vec_cols, w_cols)


def solution(mesh):
    in_specs = (P("row", "col"), P("row", None), P())
    out_specs = P("row", "col")
    return jax.shard_map(shards, mesh=mesh, in_specs=in_specs, out_specs=out_specs, check_vma=False)
```

time: 367 us -> 371 us (1.011)
  waiting for transfers between devices: 161 us -> 290 us
  matrix products: 124 us -> 14.5 us
  local copies, waits for them, and re-layouts: 64.9 us -> 3.11 us
  Pallas kernels: 0 us -> 49.1 us
    psum x2, waiting for transfers between devices: 102 us -> 178 us  [the longest x1 125 us: shards(): cross = lax.psum(inner_product(vectors, x_part), ('row', 'col'))]
    dot_general x4 -> x2, matrix products: 76.5 us -> 4.69 us  [inner_product(): lax.dot_general(left, right, TN, precision=lax.Precision.HIGHEST, preferr...]
    all_gather x2, waiting for transfers between devices: 58 us -> 110 us  [to_columns(): gathered = lax.all_gather(panel_rows, 'row', axis=0, tiled=True)]
    pallas_call x0 -> x2, Pallas kernels: none -> 49.1 us  [the longest x1 31.4 us: tile_update(): pl.pallas_call(update_kernel, grid=(rows // block,), in_specs=[pl.BlockSp...]
    dot_general x3 -> x5, matrix products: 47.1 us -> 9.82 us  [product(): jnp.dot(left, right, precision=lax.Precision.HIGHEST, preferred_element_t...]
    unnamed x9 -> x10, local copies, waits for them, and re-layouts: 33.8 us -> 0.02 us
    sub x1 -> x0, local copies, waits for them, and re-layouts: 31.1 us -> none  [shards(): matrix - outer_product(vectors, w_cols) - outer_product(w_rows, vec_cols)]
  transfers between devices with their start and end apart: 4 -> 4, of which waited for: 3 -> 4; matrix products, arithmetic and copies ran while one was open for 18% -> 1% of each run, Pallas kernels for 0% -> 0%
where the time goes in v1:
time: 371 us; the launch traced here: 370 us
  waiting for transfers between devices  290 us (78%)
  Pallas kernels  49.1 us (13%)
  matrix products  14.5 us (4%)
  between operations  13.2 us (4%)
    psum x1, waiting for transfers between devices, shards(): cross = lax.psum(inner_product(vectors, x_part), ('row', 'col'))  125 us
    all_gather x2, waiting for transfers between devices, to_columns(): gathered = lax.all_gather(panel_rows, 'row', axis=0, tiled=True)  110 us
    psum x1, waiting for transfers between devices, shards(): x_rows = lax.psum(x_part, 'col')  53.1 us
    pallas_call x1, Pallas kernels, tile_update(): pl.pallas_call(update_kernel, grid=(rows // block,), in_specs=[pl.BlockSp...  31.4 us
    pallas_call x1, Pallas kernels, tile_product(): pl.pallas_call(product_kernel, grid=(rows // block,), in_specs=[pl.BlockS...  17.7 us
    dot_general x5, matrix products, product(): jnp.dot(left, right, precision=lax.Precision.HIGHEST, preferred_element_t...  9.82 us
  transfers between devices with their start and end apart: 4, of which 4 were waited for; matrix products, arithmetic and copies ran while one was open for 1% of the time, Pallas kernels for 0%

profile of v1, /device:TPU:3, one launch (start us, length us, event | category | flops | bytes accessed | tf_op | source)
XLA Modules:
  0.0 369.9 jit_solution(7250234862971608553)
XLA Ops:
  6.5 0.0 copy-start
  6.5 0.0 all-gather.3.cloned.1.call-start
  6.5 0.7 all-gather.3.cloned.1.call-update
  7.3 58.1 %all-gather.3.cloned.1.call-done = f32[16384,128]{1,0:T(8,128)} async-done(((f32[2048,128]{1,0:T(8,128)}), f32[16384,128]{1,0:T(8,128)}) %all-gather.3.cloned.1.call-update) | async-done | bytes 8388624 | tf_op jit(solution)/shard_map/all_gather | solution.py:112
  65.3 3.1 constant_dynamic-slice_fusion.v_ref.vc_ref
  68.4 17.7 %tile_product.1 = f32[2048,128]{1,0:T(8,128)} custom-call(f32[2048,4096]{1,0:T(8,128)} %a_ref.3, f32[4096,128]{1,0:T(8,128)} %constant_dynamic-slice_fusion.v_ref.vc_ref), custom_call_target="tpu_custom_call" | custom-call | tf_op jit(solution)/shard_map/tile_product/pallas_call | solution.py:49
  86.1 0.0 copy-done.3
  86.1 3.7 convolution_bitcast_fusion.1
  89.7 0.0 all-reduce.3.cloned.1.call-start
  89.7 0.7 all-reduce.3.cloned.1.call-update
  90.5 0.0 all-reduce.5.cloned.1.call-start
  90.5 0.7 all-reduce.5.cloned.1.call-update
  91.2 0.2 all-gather.5.cloned.1.call-start
  91.4 53.1 %all-reduce.3.cloned.1.call-done = f32[2048,128]{1,0:T(8,128)} async-done(((f32[2048,128]{1,0:T(8,128)}), f32[2048,128]{1,0:T(8,128)}) %all-reduce.3.cloned.1.call-update) | async-done | bytes 1048592 | tf_op jit(solution)/shard_map/psum | solution.py:121
  144.6 0.0 all-gather.5.cloned.1.call-update
  144.6 124.9 %all-reduce.5.cloned.1.call-done = f32[128,128]{0,1:T(8,128)} async-done(((f32[128,128]{0,1:T(8,128)}), f32[128,128]{0,1:T(8,128)}) %all-reduce.5.cloned.1.call-update) | async-done | bytes 65552 | tf_op jit(solution)/shard_map/psum | solution.py:122
  269.6 1.0 fusion.5
  270.6 0.3 convolution_multiply_fusion
  270.9 1.0 fusion.4
  271.9 2.0 fusion.wr_ref
  273.9 51.5 %all-gather.5.cloned.1.call-done = f32[16384,128]{1,0:T(8,128)} async-done(((f32[2048,128]{1,0:T(8,128)}), f32[16384,128]{1,0:T(8,128)}) %all-gather.5.cloned.1.call-update) | async-done | bytes 8388624 | tf_op jit(solution)/shard_map/all_gather | solution.py:112
  325.4 3.5 fusion.1
  328.9 3.1 convolution_subtract_fusion.wc_ref
  332.0 31.4 %tile_update.1 = f32[2048,4096]{1,0:T(8,128)} custom-call(f32[2048,4096]{1,0:T(8,128)} %a_ref.3, f32[2048,128]{1,0:T(8,128)} %vr_ref.1, f32[2048,128]{1,0:T(8,128)} %fusion.wr_ref, f32[4096,128]{1,0:T(8,128)} %constant_dynamic-slice_fusion.v_ref.vc_ref, f32[4096,128]{1,0:T(8,128)} %convolution_subtract_fusion.wc_ref), custom_call_target="tpu_custom_call" | custom-call | tf_op jit(solution)/shard_map/tile_update/pallas_call | solution.py:91
  (8 shorter events, 0.0 us)
Async XLA Ops:
  6.5 263.0 %copy-start = (f32[128,128]{1,0:T(8,128)S(1)}, f32[128,128]{1,0:T(8,128)}, u32[]{:S(2)}) copy-start(f32[128,128]{1,0:T(8,128)} %param.5) | copy-start | bytes 196612
  6.5 58.8 %all-gather.3.cloned.1.call-start = ((), (), s32[]{:S(2)}) async-start(), calls=%async_computation | async-start | bytes 9437184 | tf_op jit(solution)/shard_map/all_gather | solution.py:112
  68.4 17.7 %copy-start.3 = (f32[2048,128]{1,0:T(8,128)S(1)}, f32[2048,128]{1,0:T(8,128)}, u32[]{:S(2)}) copy-start(f32[2048,128]{1,0:T(8,128)} %vr_ref.1) | copy-start | bytes 3145732
  89.7 54.8 %all-reduce.3.cloned.1.call-start = ((), (), s32[]{:S(2)}) async-start(), calls=%async_computation.1 | async-start | bytes 2097152 | tf_op jit(solution)/shard_map/psum | solution.py:121
  90.5 179.1 %all-reduce.5.cloned.1.call-start = ((), (), s32[]{:S(2)}) async-start(), calls=%async_computation.2 | async-start | bytes 131072 | tf_op jit(solution)/shard_map/psum | solution.py:122
  91.2 234.2 %all-gather.5.cloned.1.call-start = ((), (), s32[]{:S(2)}) async-start(), calls=%async_computation.3 | async-start | bytes 9437184 | tf_op jit(solution)/shard_map/all_gather | solution.py:112
  144.6 126.3 %copy-start.4 = (f32[2048,128]{1,0:T(8,128)S(1)}, f32[2048,128]{1,0:T(8,128)}, u32[]{:S(2)}) copy-start(f32[2048,128]{1,0:T(8,128)} %all-reduce.3.cloned.1.call-done) | copy-start | bytes 3145732
  273.9 55.0 %copy-start.2 = (f32[4096,128]{1,0:T(8,128)S(1)}, f32[4096,128]{1,0:T(8,128)}, u32[]{:S(2)}) copy-start(f32[4096,128]{1,0:T(8,128)} %constant_dynamic-slice_fusion.v_ref.vc_ref) | copy-start | bytes 6291460
  332.0 31.4 %copy-start.1 = (f32[128,128]{1,0:T(8,128)S(1)}, f32[128,128]{1,0:T(8,128)}, u32[]{:S(2)}) copy-start(f32[128,128]{1,0:T(8,128)} %param.5) | copy-start | bytes 196612
Sparse Core Ops, SparseCore 0:
  9.2 56.0 all-gather.2
  92.9 51.6 all-reduce.2
  151.1 118.4 all-reduce.4
  271.5 53.8 all-gather.4

commit v2 on v0

v2 whole, which is shorter than its diff:
```python
import functools

import jax
import jax.numpy as jnp
from jax import lax
from jax.experimental import pallas as pl
from jax.experimental.pallas import tpu as pltpu
from jax.sharding import PartitionSpec as P

NN = (((1,), (0,)), ((), ()))
NT = (((1,), (1,)), ((), ()))
TN = (((0,), (0,)), ((), ()))


def split(values):
    high = values.astype(jnp.bfloat16)
    low = (values - high.astype(jnp.float32)).astype(jnp.bfloat16)
    return high, low


def wide_dot(left, right, dims):
    l_high, l_low = split(left)
    r_high, r_low = split(right)
    return (
        lax.dot_general(l_high, r_high, dims, preferred_element_type=jnp.float32)
        + lax.dot_general(l_high, r_low, dims, preferred_element_type=jnp.float32)
        + lax.dot_general(l_low, r_high, dims, preferred_element_type=jnp.float32)
    )


CHUNKS = 8
LAG = 2
MESH = pl.DeviceIdType.MESH


def remote(src, dst, send_sem, recv_sem, device):
    return pltpu.make_async_remote_copy(
        src_ref=src, dst_ref=dst, send_sem=send_sem, recv_sem=recv_sem,
        device_id=device, device_id_type=MESH,
    )


def panel_kernel(
    row_count, col_count, a_hbm, v_ref, vc_out, xr_out, xc_out, g_out,
    a, vc, v2, part, rs_in, xr, xc, g_sum, g_in,
    a_sem, out_sem, v_ring_s, v_ring_r, v_sib_s, v_sib_r, x_ring_s, x_ring_r, x_sib_s, x_sib_r,
    rs_s, rs_r, ag_s, ag_r, g_s, g_r,
):
    m, nb = v_ref.shape
    half = m // 2
    chunk = half // CHUNKS
    chips = row_count // 2
    sources = chips // col_count
    last = col_count - 1
    wide = 1
    while wide * wide < chips:
        wide *= 2

    row, col = lax.axis_index("row"), lax.axis_index("col")
    chip, core = row // 2, row % 2

    def snake(at):
        y, x = at // wide, at % wide
        return y * wide + x + (y % 2) * (wide - 1 - 2 * x)

    place = snake(chip)
    sibling = (row + 1 - 2 * core, col)
    onward = (snake((place + 1) % chips) * 2 + core, col)
    backward = (snake((place + chips - 1) % chips) * 2 + core, col)
    ring = (onward, backward)
    right, left = (row, (col + 1) % col_count), (row, (col + last) % col_count)
    pairs = []
    bit = 1
    while bit < row_count:
        pairs.append((row + (1 - 2 * ((row // bit) % 2)) * bit, col))
        bit *= 2
    bit = 1
    while bit < col_count:
        pairs.append((row, col + (1 - 2 * ((col // bit) % 2)) * bit))
        bit *= 2

    def slab(h, i):
        return pl.ds(pl.multiple_of(h * half + i * chunk, chunk), chunk)

    def load(h, i):
        return pltpu.make_async_copy(a_hbm.at[slab(h, i)], a.at[slab(h, i)], a_sem.at[h, i])

    @pl.loop(0, CHUNKS)
    def _(i):
        load(0, i).start()
        load(1, i).start()

    barrier = pltpu.get_barrier_semaphore()
    greeted = [sibling, onward, backward, right, left] + pairs
    for device in greeted:
        pl.semaphore_signal(barrier, inc=1, device_id=device, device_id_type=MESH)
    pl.semaphore_wait(barrier, len(greeted))

    def distances(s):
        start = snake(col * sources + s)
        return (place - start + chips) % chips, (start - place + chips) % chips

    def block(s, whose, h, i):
        return pl.ds(pl.multiple_of((2 * s + whose) * m + h * half + i * chunk, chunk), chunk)

    def ring_copy(buf, sems, s, h, i):
        at = buf.at[block(s, core, h, i)]
        return remote(at, at, sems[0].at[s, h, i], sems[1].at[s, h, i], ring[h])

    def sib_copy(buf, sems, s, h, i, whose):
        at = buf.at[block(s, whose, h, i)]
        return remote(at, at, sems[2].at[s, h, i], sems[3].at[s, h, i], sibling)

    def spread(buf, sems, s, h, step):
        away = distances(s)[h]
        i = step - LAG * away
        live = (i >= 0) & (i < CHUNKS)

        @pl.when(live & (away > 0))
        def _():
            ring_copy(buf, sems, s, h, i).wait_recv()

        @pl.when(live & (away < chips - 1))
        def _():
            ring_copy(buf, sems, s, h, i).start()

        @pl.when(live)
        def _():
            sib_copy(buf, sems, s, h, i, core).start()

    def spread_sent(buf, sems, s, h, i):
        @pl.when(distances(s)[h] < chips - 1)
        def _():
            ring_copy(buf, sems, s, h, i).wait_send()

        sib_copy(buf, sems, s, h, i, core).wait_send()

    v_sems = (v_ring_s, v_ring_r, v_sib_s, v_sib_r)
    x_sems = (x_ring_s, x_ring_r, x_sib_s, x_sib_r)

    for s in range(sources):
        @pl.when(chip == col * sources + s)
        def _():
            vc[pl.ds(pl.multiple_of((2 * s + core) * m, m), m), :] = v_ref[...]

    @pl.loop(0, CHUNKS + LAG * (chips - 1))
    def _(t):
        for s in range(sources):
            for h in range(2):
                spread(vc, v_sems, s, h, t)

    @pl.loop(0, CHUNKS)
    def _(i):
        for s in range(sources):
            for h in range(2):
                sib_copy(vc, v_sems, s, h, i, 1 - core).wait_recv()

    vc_copy = pltpu.make_async_copy(vc, vc_out, out_sem.at[0])
    vc_copy.start()

    v_high, v_low = split(vc[...])
    v2[:, :nb] = v_high
    v2[:, nb:] = v_low
    g_sum[0] = jnp.zeros((nb, nb), jnp.float32)

    def rs_copy(h, i):
        return remote(
            part.at[slab(h, i)], rs_in.at[slab(h, i)], rs_s.at[h, i], rs_r.at[h, i], (left, right)[h]
        )

    def ag_copy(h, i):
        at = xr.at[slab(h, i)]
        return remote(at, at, ag_s.at[h, i], ag_r.at[h, i], (right, left)[h])

    def g_copy(j):
        return remote(g_sum.at[j], g_in.at[j], g_s.at[j], g_r.at[j], pairs[j])

    @pl.loop(0, CHUNKS + LAG * (2 * last + chips - 1))
    def _(t):
        @pl.when(t < CHUNKS)
        def _():
            load(0, t).wait()
            load(1, t).wait()
            parts = split(a[slab(0, t), :]) + split(a[slab(1, t), :])
            both = jnp.dot(jnp.concatenate(parts, axis=0), v2[...], preferred_element_type=jnp.float32)
            both = both[:, :nb] + both[:, nb:]
            first = both[:chunk] + both[chunk : 2 * chunk]
            second = both[2 * chunk : 3 * chunk] + both[3 * chunk :]
            part[slab(0, t), :] = first
            part[slab(1, t), :] = second
            g_sum[0] += wide_dot(v_ref[slab(0, t), :], first, TN) + wide_dot(
                v_ref[slab(1, t), :], second, TN
            )

        for h in range(2):
            depth = last - col if h == 0 else col
            i = t - LAG * depth
            live = (i >= 0) & (i < CHUNKS)

            @pl.when(live & (depth > 0))
            def _():
                rs_copy(h, i).wait_recv()
                part[slab(h, i), :] += rs_in[slab(h, i), :]

            @pl.when(live & (depth < last))
            def _():
                rs_copy(h, i).start()

            @pl.when(live & (depth == last))
            def _():
                xr[slab(h, i), :] = part[slab(h, i), :]

        for h in range(2):
            far = col if h == 0 else last - col
            i = t - LAG * (last + far)
            live = (i >= 0) & (i < CHUNKS)

            @pl.when(live & (far > 0))
            def _():
                ag_copy(h, i).wait_recv()

            @pl.when(live & (far < last))
            def _():
                ag_copy(h, i).start()

            for s in range(sources):
                @pl.when(live & (chip == col * sources + s))
                def _():
                    xc[block(s, core, h, i), :] = xr[slab(h, i), :]

                spread(xc, x_sems, s, h, t - LAG * (last + far))

        for j in range(len(pairs) + 1):
            @pl.when(t == CHUNKS - 1 + LAG * j)
            def _():
                if j > 0:
                    g_copy(j - 1).wait_recv()
                    g_sum[j] = g_sum[j - 1] + g_in[j - 1]
                if j < len(pairs):
                    g_copy(j).start()

    xr_copy = pltpu.make_async_copy(xr, xr_out, out_sem.at[1])
    xr_copy.start()
    g_out[...] = g_sum[len(pairs)]

    @pl.loop(0, CHUNKS)
    def _(i):
        for s in range(sources):
            for h in range(2):
                sib_copy(xc, x_sems, s, h, i, 1 - core).wait_recv()

    xc_copy = pltpu.make_async_copy(xc, xc_out, out_sem.at[2])
    xc_copy.start()

    @pl.loop(0, CHUNKS)
    def _(i):
        for s in range(sources):
            for h in range(2):
                spread_sent(vc, v_sems, s, h, i)
                spread_sent(xc, x_sems, s, h, i)
        for h in range(2):
            depth = last - col if h == 0 else col

            @pl.when(depth < last)
            def _():
                rs_copy(h, i).wait_send()

            far = col if h == 0 else last - col

            @pl.when(far < last)
            def _():
                ag_copy(h, i).wait_send()

    for j in range(len(pairs)):
        g_copy(j).wait_send()
    vc_copy.wait()
    xr_copy.wait()
    xc_copy.wait()


def panel(matrix, vectors):
    m, n = matrix.shape
    nb = vectors.shape[1]
    rows, cols = lax.axis_size("row"), lax.axis_size("col")
    sources = rows // 2 // cols
    steps = (rows - 1).bit_length() + (cols - 1).bit_length()
    f32 = jnp.float32
    dma = pltpu.SemaphoreType.DMA
    whole = pl.BlockSpec(memory_space=pltpu.VMEM)
    hbm = pl.BlockSpec(memory_space=pl.ANY)
    return pl.pallas_call(
        functools.partial(panel_kernel, rows, cols),
        in_specs=[hbm, whole],
        out_specs=[hbm, hbm, hbm, whole],
        out_shape=[
            jax.ShapeDtypeStruct((n, nb), f32),
            jax.ShapeDtypeStruct((m, nb), f32),
            jax.ShapeDtypeStruct((n, nb), f32),
            jax.ShapeDtypeStruct((nb, nb), f32),
        ],
        scratch_shapes=[
            pltpu.VMEM((m, n), f32),
            pltpu.VMEM((n, nb), f32),
            pltpu.VMEM((n, 2 * nb), jnp.bfloat16),
            pltpu.VMEM((m, nb), f32),
            pltpu.VMEM((m, nb), f32),
            pltpu.VMEM((m, nb), f32),
            pltpu.VMEM((n, nb), f32),
            pltpu.VMEM((steps + 1, nb, nb), f32),
            pltpu.VMEM((steps, nb, nb), f32),
            dma((2, CHUNKS)),
            dma((3,)),
        ]
        + [dma((sources, 2, CHUNKS))] * 8
        + [dma((2, CHUNKS))] * 4
        + [dma((steps,))] * 2,
        compiler_params=pltpu.CompilerParams(
            collective_id=0, has_side_effects=True, vmem_limit_bytes=60 << 20
        ),
        name="panel_products",
    )(matrix, vectors)


def update_kernel(a_ref, v_ref, xr_ref, t_ref, g_ref, vc_ref, xc_ref, out_ref, right, middle):
    nb = v_ref.shape[1]
    columns = a_ref.shape[1]
    wide = min(512, columns)

    @pl.when(pl.program_id(0) == 0)
    def _():
        half = 0.5 * wide_dot(wide_dot(t_ref[...], g_ref[...], TN), t_ref[...], NN)
        middle[...] = half + half.T
        for at, ref in ((0, xc_ref), (nb, vc_ref)):
            high, low = split(ref[...])
            right[:, at : at + nb] = high
            right[:, 2 * nb + at : 3 * nb + at] = low
            right[:, 4 * nb + at : 5 * nb + at] = high

    vectors = v_ref[...]
    l_high, l_low = split(wide_dot(vectors, t_ref[...], NT))
    w_high, w_low = split(
        wide_dot(xr_ref[...], t_ref[...], NN) - wide_dot(vectors, middle[...], NN)
    )
    left = jnp.concatenate([l_high, w_high, l_high, w_high, l_low, w_low], axis=1)
    for at in range(0, columns, wide):
        change = lax.dot_general(
            left, right[at : at + wide, :], NT, preferred_element_type=jnp.float32
        )
        out_ref[:, at : at + wide] = a_ref[:, at : at + wide] - change


def tile_update(matrix, vectors, x_rows, tfactor, cross, vec_cols, x_cols):
    rows, columns = matrix.shape
    nb = vectors.shape[1]
    block = min(256, rows)
    panel_rows = pl.BlockSpec((block, nb), lambda i: (i, 0))
    small = pl.BlockSpec((nb, nb), lambda i: (0, 0))
    panel_cols = pl.BlockSpec((columns, nb), lambda i: (0, 0))
    tile = pl.BlockSpec((block, columns), lambda i: (i, 0))
    return pl.pallas_call(
        update_kernel,
        grid=(rows // block,),
        in_specs=[tile, panel_rows, panel_rows, small, small, panel_cols, panel_cols],
        out_specs=tile,
        out_shape=jax.ShapeDtypeStruct((rows, columns), jnp.float32),
        scratch_shapes=[
            pltpu.VMEM((columns, 6 * nb), jnp.bfloat16),
            pltpu.VMEM((nb, nb), jnp.float32),
        ],
        compiler_params=pltpu.CompilerParams(vmem_limit_bytes=56 << 20),
        name="tile_update",
    )(matrix, vectors, x_rows, tfactor, cross, vec_cols, x_cols)


def shards(matrix, vectors, tfactor):
    vec_cols, x_rows, x_cols, cross = panel(matrix, vectors)
    return tile_update(matrix, vectors, x_rows, tfactor, cross, vec_cols, x_cols)


def solution(mesh):
    in_specs = (P("row", "col"), P("row", None), P())
    out_specs = P("row", "col")
    return jax.shard_map(shards, mesh=mesh, in_specs=in_specs, out_specs=out_specs, check_vma=False)
```

time: 367 us -> 115 us (0.31); the launches traced: 362 us -> 115 us
  waiting for transfers between devices: 161 us -> 0 us
  matrix products: 124 us -> 0 us
  Pallas kernels: 0 us -> 115 us
  local copies, waits for them, and re-layouts: 64.9 us -> 0 us
  between operations: 13.2 us -> 0.01 us
    dot_general x7 -> x0, matrix products: 124 us -> none  [the longest x2 73 us: outer_product(): lax.dot_general(left, right, (((1,), (1,)), ((), ())), precision=lax.Prec...]
    pallas_call x0 -> x2, Pallas kernels: none -> 115 us  [the longest x1 80.5 us: panel(): pl.pallas_call(functools.partial(panel_kernel, rows, cols), in_specs=[hbm...]
    psum x2 -> x0, waiting for transfers between devices: 102 us -> none  [the longest x1 51.7 us: shards(): x_rows = lax.psum(product(matrix, vec_cols), 'col')]
    all_gather x2 -> x0, waiting for transfers between devices: 58 us -> none  [to_columns(): gathered = lax.all_gather(panel_rows, 'row', axis=0, tiled=True)]
    unnamed x9 -> x0, local copies, waits for them, and re-layouts: 33.8 us -> none
    sub x1 -> x0, local copies, waits for them, and re-layouts: 31.1 us -> none  [shards(): matrix - outer_product(vectors, w_cols) - outer_product(w_rows, vec_cols)]
  transfers between devices with their start and end apart: 4 -> 0, of which waited for: 3 -> 0; matrix products, arithmetic and copies ran while one was open for 18% -> 0% of each run, Pallas kernels for 0% -> 0%
where the time goes in v2:
time: 115 us
  Pallas kernels  115 us (100%)
    pallas_call x1, Pallas kernels, panel(): pl.pallas_call(functools.partial(panel_kernel, rows, cols), in_specs=[hbm...  80.5 us
    pallas_call x1, Pallas kernels, tile_update(): pl.pallas_call(update_kernel, grid=(rows // block,), in_specs=[tile, pane...  34.1 us

profile of v2, /device:TPU:3, one launch (start us, length us, event | category | flops | bytes accessed | tf_op | source)
XLA Modules:
  0.0 114.6 jit_solution(3282661706093722597)
XLA Ops:
  0.0 80.5 %panel_products.1 = (f32[4096,128]{1,0:T(8,128)}, f32[2048,128]{1,0:T(8,128)}, f32[4096,128]{1,0:T(8,128)}, f32[128,128]{1,0:T(8,128)}) custom-call(f32[2048,4096]{1,0:T(8,128)} %a_ref.1, f32[2048,128]{1,0:T(8,128)} %v_ref.3), custom_call_target="tpu_custom_call" | custom-call | tf_op jit(solution)/shard_map/panel_products/pallas_call | solution.py:291
  80.5 34.1 %tile_update.1 = f32[2048,4096]{1,0:T(8,128)} custom-call(f32[2048,4096]{1,0:T(8,128)} %a_ref.1, f32[2048,128]{1,0:T(8,128)} %v_ref.3, f32[2048,128]{1,0:T(8,128)} %get-tuple-element.9.xr_ref, f32[128,128]{1,0:T(8,128)} %t_ref.1, f32[128,128]{1,0:T(8,128)} %get-tuple-element.10.g_ref, f32[4096,128]{1,0:T(8,128)} %get-tuple-element.11.vc_ref, ...), custom_call_target="tpu_custom_call" | custom-call | tf_op jit(solution)/shard_map/tile_update/pallas_call | solution.py:360

commit v3 on v2

--- a/solution.py
+++ b/solution.py
@@ -321,52 +321,45 @@
     )(matrix, vectors)
 
 
-def update_kernel(a_ref, v_ref, xr_ref, t_ref, g_ref, vc_ref, xc_ref, out_ref, right, middle):
-    nb = v_ref.shape[1]
-    columns = a_ref.shape[1]
-    wide = min(512, columns)
+def update_kernel(a_ref, v_ref, xr_ref, t_ref, g_ref, vc_ref, xc_ref, out_ref, left):
+    rows = a_ref.shape[0]
+    tall = min(1024, rows)
 
     @pl.when(pl.program_id(0) == 0)
     def _():
         half = 0.5 * wide_dot(wide_dot(t_ref[...], g_ref[...], TN), t_ref[...], NN)
-        middle[...] = half + half.T
-        for at, ref in ((0, xc_ref), (nb, vc_ref)):
-            high, low = split(ref[...])
-            right[:, at : at + nb] = high
-            right[:, 2 * nb + at : 3 * nb + at] = low
-            right[:, 4 * nb + at : 5 * nb + at] = high
-
-    vectors = v_ref[...]
-    l_high, l_low = split(wide_dot(vectors, t_ref[...], NT))
-    w_high, w_low = split(
-        wide_dot(xr_ref[...], t_ref[...], NN) - wide_dot(vectors, middle[...], NN)
-    )
-    left = jnp.concatenate([l_high, w_high, l_high, w_high, l_low, w_low], axis=1)
-    for at in range(0, columns, wide):
+        vectors = v_ref[...]
+        l_high, l_low = split(wide_dot(vectors, t_ref[...], NT))
+        w_high, w_low = split(
+            wide_dot(xr_ref[...], t_ref[...], NN) - wide_dot(vectors, half + half.T, NN)
+        )
+        left[...] = jnp.concatenate([l_high, w_high, l_high, w_high, l_low, w_low], axis=1)
+
+    x_high, x_low = split(xc_ref[...])
+    v_high, v_low = split(vc_ref[...])
+    right = jnp.concatenate([x_high, v_high, x_low, v_low, x_high, v_high], axis=1)
+    for at in range(0, rows, tall):
         change = lax.dot_general(
-            left, right[at : at + wide, :], NT, preferred_element_type=jnp.float32
+            left[at : at + tall, :], right, NT, preferred_element_type=jnp.float32
         )
-        out_ref[:, at : at + wide] = a_ref[:, at : at + wide] - change
+        out_ref[at : at + tall, :] = a_ref[at : at + tall, :] - change
 
 
 def tile_update(matrix, vectors, x_rows, tfactor, cross, vec_cols, x_cols):
     rows, columns = matrix.shape
     nb = vectors.shape[1]
-    block = min(256, rows)
-    panel_rows = pl.BlockSpec((block, nb), lambda i: (i, 0))
+    block = min(256, columns)
+    panel_rows = pl.BlockSpec((rows, nb), lambda i: (0, 0))
     small = pl.BlockSpec((nb, nb), lambda i: (0, 0))
-    panel_cols = pl.BlockSpec((columns, nb), lambda i: (0, 0))
-    tile = pl.BlockSpec((block, columns), lambda i: (i, 0))
+    panel_cols = pl.BlockSpec((block, nb), lambda i: (i, 0))
+    tile = pl.BlockSpec((rows, block), lambda i: (0, i))
     return pl.pallas_call(
         update_kernel,
-        grid=(rows // block,),
+        grid=(columns // block,),
         in_specs=[tile, panel_rows, panel_rows, small, small, panel_cols, panel_cols],
         out_specs=tile,
         out_shape=jax.ShapeDtypeStruct((rows, columns), jnp.float32),
-        scratch_shapes=[
-            pltpu.VMEM((columns, 6 * nb), jnp.bfloat16),
-            pltpu.VMEM((nb, nb), jnp.float32),
-        ],
+        scratch_shapes=[pltpu.VMEM((rows, 6 * nb), jnp.bfloat16)],
         compiler_params=pltpu.CompilerParams(vmem_limit_bytes=56 << 20),
         name="tile_update",
     )(matrix, vectors, x_rows, tfactor, cross, vec_cols, x_cols)

time: 115 us -> 118 us (1.026)
  Pallas kernels: 115 us -> 117 us
    pallas_call x1, Pallas kernels: 34.1 us -> 36.8 us  [tile_update(): pl.pallas_call(update_kernel, grid=(columns // block,), in_specs=[tile, p...]
where the time goes in v3:
time: 118 us; the launch traced here: 117 us
  Pallas kernels  117 us (99%)
    pallas_call x1, Pallas kernels, panel(): pl.pallas_call(functools.partial(panel_kernel, rows, cols), in_specs=[hbm...  80.5 us
    pallas_call x1, Pallas kernels, tile_update(): pl.pallas_call(update_kernel, grid=(columns // block,), in_specs=[tile, p...  36.8 us

profile of v3, /device:TPU:3, one launch (start us, length us, event | category | flops | bytes accessed | tf_op | source)
XLA Modules:
  0.0 117.3 jit_solution(17011949350548460559)
XLA Ops:
  0.0 80.5 %panel_products.1 = (f32[4096,128]{1,0:T(8,128)}, f32[2048,128]{1,0:T(8,128)}, f32[4096,128]{1,0:T(8,128)}, f32[128,128]{1,0:T(8,128)}) custom-call(f32[2048,4096]{1,0:T(8,128)} %a_ref.1, f32[2048,128]{1,0:T(8,128)} %v_ref.3), custom_call_target="tpu_custom_call" | custom-call | tf_op jit(solution)/shard_map/panel_products/pallas_call | solution.py:291
  80.5 36.8 %tile_update.1 = f32[2048,4096]{1,0:T(8,128)} custom-call(f32[2048,4096]{1,0:T(8,128)} %a_ref.1, f32[2048,128]{1,0:T(8,128)} %v_ref.3, f32[2048,128]{1,0:T(8,128)} %get-tuple-element.9.xr_ref, f32[128,128]{1,0:T(8,128)} %t_ref.1, f32[128,128]{1,0:T(8,128)} %get-tuple-element.10.g_ref, f32[4096,128]{1,0:T(8,128)} %get-tuple-element.11.vc_ref, ...), custom_call_target="tpu_custom_call" | custom-call | tf_op jit(solution)/shard_map/tile_update/pallas_call | solution.py:356

commit v4 on v2

--- a/solution.py
+++ b/solution.py
@@ -29,7 +29,7 @@
 
 
 CHUNKS = 8
-LAG = 2
+LAG = 3
 MESH = pl.DeviceIdType.MESH
 
 

time: 115 us -> 116 us (level)
  no operation moved by 1% of the time
where the time goes in v4:
time: 116 us
  Pallas kernels  116 us (100%)
    pallas_call x1, Pallas kernels, panel(): pl.pallas_call(functools.partial(panel_kernel, rows, cols), in_specs=[hbm...  81.5 us
    pallas_call x1, Pallas kernels, tile_update(): pl.pallas_call(update_kernel, grid=(rows // block,), in_specs=[tile, pane...  34.1 us

profile of v4, /device:TPU:3, one launch (start us, length us, event | category | flops | bytes accessed | tf_op | source)
XLA Modules:
  0.0 115.6 jit_solution(14360519753721639984)
XLA Ops:
  0.0 81.5 %panel_products.1 = (f32[4096,128]{1,0:T(8,128)}, f32[2048,128]{1,0:T(8,128)}, f32[4096,128]{1,0:T(8,128)}, f32[128,128]{1,0:T(8,128)}) custom-call(f32[2048,4096]{1,0:T(8,128)} %a_ref.1, f32[2048,128]{1,0:T(8,128)} %v_ref.3), custom_call_target="tpu_custom_call" | custom-call | tf_op jit(solution)/shard_map/panel_products/pallas_call | solution.py:291
  81.5 34.1 %tile_update.1 = f32[2048,4096]{1,0:T(8,128)} custom-call(f32[2048,4096]{1,0:T(8,128)} %a_ref.1, f32[2048,128]{1,0:T(8,128)} %v_ref.3, f32[2048,128]{1,0:T(8,128)} %get-tuple-element.9.xr_ref, f32[128,128]{1,0:T(8,128)} %t_ref.1, f32[128,128]{1,0:T(8,128)} %get-tuple-element.10.g_ref, f32[4096,128]{1,0:T(8,128)} %get-tuple-element.11.vc_ref, ...), custom_call_target="tpu_custom_call" | custom-call | tf_op jit(solution)/shard_map/tile_update/pallas_call | solution.py:360
